TPU v7x, 32 devices: a whole 2x2x4 slice. The times are simulated.
32 devices in a mesh: groups: 2 (over y), tiles: 8 (over z, x), comp: 2 (over core).
Axes of the slice: x: 2, y: 2, z: 4, core: 2. Of those that a mesh axis runs over, the one named last changes fastest.
Arguments:
- state_field: bfloat16 [2, 384, 16384], P('comp', None, ('groups', 'tiles')), parts along dimension 2, may hold values from -6 to 6
- cotangent: bfloat16 [2, 384, 16384], P('comp', None, ('groups', 'tiles')), parts along dimension 2, may hold values from -6 to 6
- w_in: bfloat16 [2, 384, 1536], P('comp'), may hold values from -0.3125 to 0.3125
- w_out: bfloat16 [2, 1536, 384], P('comp'), may hold values from -0.15625 to 0.15625
- norm_gain: float32 [2, 384], P('comp'), may hold values from 0.5 to 1.5
- export_weight: bfloat16 [2, 8, 384], P('comp'), may hold values from -0.3125 to 0.3125
- lift_weight: float32 [2, 384, 8], P('comp'), may hold values from -2 to 2
- wet_mask: int32 [16384], P(('groups', 'tiles')), parts along dimension 0, may hold values 0 or 1
- remap_tile: int32 [2, 512, 1], P('comp', 'tiles'), may hold values from 0 to 7; in each aligned block of 64 rows (0 to 63, 64 to 127, ..., all dimensions but the last counted through in order) at most 16 rows name the same one
- source_block: int32 [2, 512], P('comp', 'tiles'), may hold values from 0 to 7
- target_block: int32 [2, 512], P('comp', 'tiles'), may hold values from 0 to 7
- slot_alive: int32 [2, 512], P('comp', 'tiles'), may hold values 0 or 1
- remap_weights: bfloat16 [2, 512, 128, 128], P('comp', 'tiles'), may hold values from -0.5 to 0.5
Outputs:
- grad_state: float32 [2, 384, 16384], P('comp', None, ('groups', 'tiles')), parts along dimension 2
- grad_w_in: float32 [4, 384, 1536], P(('groups', 'comp')), parts along dimension 0
- grad_w_out: float32 [4, 1536, 384], P(('groups', 'comp')), parts along dimension 0
- grad_gain: float32 [4, 384], P(('groups', 'comp')), parts along dimension 0
- grad_export: float32 [4, 8, 384], P(('groups', 'comp')), parts along dimension 0
- grad_lift: float32 [4, 384, 8], P(('groups', 'comp')), parts along dimension 0
There are 2 independent parts, one for each index of `groups`. A program takes and returns all parts, laid end to end along the dimension named above; an argument that names none is the same for every part. Nothing has to cross between parts.
Inputs may be any that keep to these rules, and one draw needn't show every extreme that they name: `remap_tile`: at most 16 slots of one tile of a component name the same target tile, and some tile reaches that bound.
All inputs are finite; a program needn't handle non-finite values. No bound on the sum of `wet_mask` or of `slot_alive` on one device may be relied on, other than what follows from the above.
Results may differ from a plain program's by a relative error of at most 0.0057.
Values may be sent and summed in bfloat16 or wider, within the bound.
A program may use at most 64 MiB of HBM per device.

v0:
```python
import jax
import jax.numpy as jnp
from jax import lax
from jax.sharding import PartitionSpec as P

norm_eps = 1e-05
highest = lax.Precision.HIGHEST


def swapped(value, axis, distance):
    mask = 2**distance
    pairs = [(source, source ^ mask) for source in range(lax.axis_size(axis))]
    return lax.ppermute(value, axis, pairs)


def gelu_parts(hidden):
    inner = 0.7978845608 * (hidden + 0.044715 * hidden * hidden * hidden)
    tanh_inner = jnp.tanh(inner)
    gelu_value = 0.5 * hidden * (1.0 + tanh_inner)
    gelu_slope = 0.5 * (1.0 + tanh_inner) + 0.5 * hidden * (
        1.0 - tanh_inner * tanh_inner
    ) * 0.7978845608 * (1.0 + 0.134145 * hidden * hidden)
    return (gelu_value, gelu_slope)


def slots_across_tiles(values, block_ids):
    return (
        lax.all_to_all(values, "tiles", split_axis=0, concat_axis=0, tiled=True),
        lax.all_to_all(block_ids, "tiles", split_axis=0, concat_axis=0, tiled=True),
    )


def slots_across_comp(values, block_ids):
    return swapped((values, block_ids), "comp", 0)


def adjoint_across_tiles(values):
    return lax.all_to_all(values, "tiles", split_axis=0, concat_axis=0, tiled=True)


def adjoint_across_comp(values):
    return swapped(values, "comp", 0)


def body(
    state_field,
    cotangent,
    w_in,
    w_out,
    norm_gain,
    export_weight,
    lift_weight,
    wet_mask,
    remap_tile,
    source_block,
    target_block,
    slot_alive,
    remap_weights,
):
    tile_count = lax.axis_size("tiles")
    state_local = state_field[0]
    cotangent_local = cotangent[0]
    w_in_local = w_in[0]
    w_out_local = w_out[0]
    gain_local = norm_gain[0]
    export_local = export_weight[0]
    lift_local = lift_weight[0]
    weights_local = remap_weights[0]
    targets = remap_tile[0, :, 0]
    source_local = source_block[0]
    target_local = target_block[0]
    alive_local = slot_alive[0].astype(jnp.float32)
    channels, cell_count = state_local.shape
    field_count = export_local.shape[0]
    block_width = weights_local.shape[-1]
    block_count = cell_count // block_width
    slot_count = weights_local.shape[0]
    capacity = max(2, 2 * slot_count // tile_count)
    spot_count = tile_count * capacity
    exported = jnp.dot(export_local, state_local, preferred_element_type=jnp.float32).astype(
        jnp.bfloat16
    )
    pick_source = source_local[:, None] == jnp.arange(block_count, dtype=jnp.int32)[None, :]
    source_rows = jnp.einsum(
        "lb,kbp->lkp",
        pick_source.astype(jnp.bfloat16),
        exported.reshape(field_count, block_count, block_width),
        preferred_element_type=jnp.float32,
    ).astype(jnp.bfloat16)
    products = (
        jnp.einsum("lkp,lqp->lkq", source_rows, weights_local, preferred_element_type=jnp.float32)
        * alive_local[:, None, None]
    )
    to_tile = (targets[:, None] == jnp.arange(tile_count, dtype=jnp.int32)[None, :]).astype(
        jnp.int32
    )
    earlier = jnp.cumsum(to_tile, axis=0) - to_tile
    slot_rank = jnp.sum(earlier * to_tile, axis=1)
    position = targets * capacity + slot_rank
    placing = position[None, :] == jnp.arange(spot_count, dtype=jnp.int32)[:, None]
    outgoing = jnp.einsum("sl,lkq->skq", placing.astype(jnp.float32), products, precision=highest)
    outgoing_ids = jnp.sum(placing.astype(jnp.int32) * target_local[None, :], axis=1)
    middle, middle_ids = slots_across_comp(outgoing, outgoing_ids)
    incoming, incoming_ids = slots_across_tiles(middle, middle_ids)
    pick_target = incoming_ids[:, None] == jnp.arange(block_count, dtype=jnp.int32)[None, :]
    forcing = jnp.einsum(
        "sb,skq->kbq", pick_target.astype(jnp.float32), incoming, precision=highest
    ).reshape(field_count, cell_count)
    summed_in = state_local.astype(jnp.float32) + jnp.dot(
        lift_local, forcing, precision=highest, preferred_element_type=jnp.float32
    )
    centre = summed_in - jnp.mean(summed_in, axis=0, keepdims=True)
    variance = jnp.mean(centre * centre, axis=0, keepdims=True)
    inv_std = 1.0 / jnp.sqrt(variance + norm_eps)
    normed = centre * inv_std
    scaled = (gain_local[:, None] * normed).astype(jnp.bfloat16)
    hidden = jnp.einsum("ch,cp->hp", w_in_local, scaled, preferred_element_type=jnp.float32)
    gelu_value, gelu_slope = gelu_parts(hidden)
    active = gelu_value.astype(jnp.bfloat16)
    is_ocean = lax.axis_index("comp") == 1
    wet_factor = jnp.where(is_ocean, wet_mask, jnp.ones_like(wet_mask))
    masked = jnp.where(wet_factor[None, :] > 0, cotangent_local, jnp.zeros_like(cotangent_local))
    d_active = jnp.dot(w_out_local, masked, preferred_element_type=jnp.float32)
    g_out = jnp.einsum("hp,cp->hc", active, masked, preferred_element_type=jnp.float32)
    d_hidden = (d_active * gelu_slope).astype(jnp.bfloat16)
    g_in = jnp.einsum("cp,hp->ch", scaled, d_hidden, preferred_element_type=jnp.float32)
    d_scaled = jnp.dot(w_in_local, d_hidden, preferred_element_type=jnp.float32)
    g_gain = jnp.sum(d_scaled * normed, axis=1)
    weighted = d_scaled * gain_local[:, None]
    d_summed = inv_std * (
        weighted
        - jnp.mean(weighted, axis=0, keepdims=True)
        - normed * jnp.mean(weighted * normed, axis=0, keepdims=True)
    ) + masked.astype(jnp.float32)
    g_lift = jnp.einsum(
        "cp,kp->ck", d_summed, forcing, precision=highest, preferred_element_type=jnp.float32
    )
    d_forcing = jnp.einsum(
        "ck,cp->kp", lift_local, d_summed, precision=highest, preferred_element_type=jnp.float32
    ).astype(jnp.bfloat16)
    returning = jnp.einsum(
        "sb,kbq->skq",
        pick_target.astype(jnp.bfloat16),
        d_forcing.reshape(field_count, block_count, block_width),
        preferred_element_type=jnp.float32,
    ).astype(jnp.bfloat16)
    returned = adjoint_across_comp(adjoint_across_tiles(returning))
    slot_force = jnp.einsum(
        "sl,skq->lkq", placing.astype(jnp.bfloat16), returned, preferred_element_type=jnp.float32
    ).astype(jnp.bfloat16)
    pulled = (
        jnp.einsum("lkq,lqp->lkp", slot_force, weights_local, preferred_element_type=jnp.float32)
        * alive_local[:, None, None]
    )
    d_exported = (
        jnp.einsum("lb,lkp->kbp", pick_source.astype(jnp.float32), pulled, precision=highest)
        .reshape(field_count, cell_count)
        .astype(jnp.bfloat16)
    )
    g_export = jnp.einsum("kp,cp->kc", d_exported, state_local, preferred_element_type=jnp.float32)
    grad_local = d_summed + jnp.einsum(
        "kc,kp->cp", export_local, d_exported, preferred_element_type=jnp.float32
    )
    g_in, g_out, g_gain, g_export, g_lift = lax.psum(
        (g_in, g_out, g_gain, g_export, g_lift), "tiles"
    )
    return (grad_local[None], g_in[None], g_out[None], g_gain[None], g_export[None], g_lift[None])


def solution(mesh):
    placed = (
        P("comp", None, ("groups", "tiles")),
        P("comp", None, ("groups", "tiles")),
        P("comp", None, None),
        P("comp", None, None),
        P("comp", None),
        P("comp", None, None),
        P("comp", None, None),
        P(("groups", "tiles")),
        P("comp", "tiles", None),
        P("comp", "tiles"),
        P("comp", "tiles"),
        P("comp", "tiles"),
        P("comp", "tiles", None, None),
    )
    return jax.shard_map(
        body,
        mesh=mesh,
        in_specs=placed,
        out_specs=(
            P("comp", None, ("groups", "tiles")),
            P(("groups", "comp"), None, None),
            P(("groups", "comp"), None, None),
            P(("groups", "comp"), None),
            P(("groups", "comp"), None, None),
            P(("groups", "comp"), None, None),
        ),
        check_vma=False,
    )
```

profile of v0, /device:TPU:0, one launch (start us, length us, event | category | flops | bytes accessed | tf_op | source)
XLA Modules:
  0.0 251.6 jit_solution(6784917680908396771)
XLA Ops:
  7.2 0.8 convert_bitcast_fusion
  8.0 0.7 fusion.48
  8.7 0.1 reduce_window_sum.11
  8.8 0.8 select_reduce_fusion.1
  9.7 0.7 multiply_add_fusion.1
  10.3 1.4 fusion.28
  11.7 0.9 convolution_convert_fusion.2
  12.6 1.2 fusion.21
  13.8 0.5 fusion.39
  14.3 0.5 collective-permute-start
  14.8 0.1 select_reduce_fusion
  14.9 0.1 collective-permute-start.1
  15.0 1.3 collective-permute-done.1
  16.4 0.7 all_to_all.13
  17.0 7.1 %all-to-all-start.1 = ((s32[8,16,1]{1,2,0:T(1,128)}), s32[8,16,1]{1,2,0:T(1,128)S(1)}, u32[]{:S(2)}, u32[]{:S(2)}) async-start(s32[8,16,1]{1,2,0:T(1,128)} %bitcast.10), calls=%async_computation.1 | async-start | bytes 8192 | tf_op jit(solution)/shard_map/all_to_all | solution.py:29
  24.2 2.1 copy.36
  26.3 4.2 %all-to-all-done.1 = s32[8,16,1]{1,2,0:T(1,128)S(1)} async-done(((s32[8,16,1]{1,2,0:T(1,128)}), s32[8,16,1]{1,2,0:T(1,128)S(1)}, u32[]{:S(2)}, u32[]{:S(2)}) %all-to-all-start.1) | async-done | bytes 544 | tf_op jit(solution)/shard_map/all_to_all | solution.py:29
  30.6 3.5 %all-to-all-start = ((f32[128,8,128]{2,1,0:T(8,128)}), f32[128,8,128]{2,1,0:T(8,128)S(1)}, u32[]{:S(2)}, u32[]{:S(2)}) async-start(f32[128,8,128]{2,1,0:T(8,128)} %copy.36), calls=%async_computation | async-start | bytes 1048576 | tf_op jit(solution)/shard_map/all_to_all | solution.py:28
  34.1 0.2 all-reduce.4.cloned.1.call-start
  34.3 0.5 broadcast.91
  34.9 0.7 reduce.4
  35.5 0.1 eq.69
  35.6 12.1 %all-to-all-done = f32[128,8,128]{2,1,0:T(8,128)S(1)} async-done(((f32[128,8,128]{2,1,0:T(8,128)}), f32[128,8,128]{2,1,0:T(8,128)S(1)}, u32[]{:S(2)}, u32[]{:S(2)}) %all-to-all-start) | async-done | bytes 524320 | tf_op jit(solution)/shard_map/all_to_all | solution.py:28
  47.7 0.3 convolution_bitcast_fusion.1
  48.0 1.5 fusion.79
  49.6 0.2 multiply_reduce_fusion.1
  49.9 1.9 fusion.18
  51.8 3.5 %fusion.8 = f32[1,1536,384]{2,1,0:T(8,128)} fusion(f32[1024,1536]{1,0:T(8,128)S(1)} %fusion.18, bf16[1,384,1024]{2,1,0:T(8,128)(2,1)S(1)} %copy-done.7, pred[1024]{0:T(1024)(128)(4,1)S(1)} %select_compare_fusion), kind=kOutput, calls=%fused_computation.13 | convolution fusion | flops 1222508544 | bytes 9438208 | tf_op jit(solution)/shard_map/hp,cp->hc/dot_general | solution.py:124
  55.3 4.9 %fusion.6 = bf16[1536,1024]{0,1:T(8,128)(2,1)S(1)} fusion(f32[1024,1536]{1,0:T(8,128)S(1)} %fusion.18, bf16[1,1536,384]{2,1,0:T(8,128)(2,1)S(1)} %copy-done.14, bf16[1,384,1024]{2,1,0:T(8,128)(2,1)S(1)} %copy-done.7, pred[1024]{0:T(1024)(128)(4,1)S(1)} %select_compare_fusion), kind=kOutput, calls=%fused_computation.8 | convolution fusion | flops 1238237184 | bytes 11404288 | tf_op jit(solution)/shard_map/dot_general | solution.py:123
  60.3 1.7 copy-done.16
  62.0 2.8 %convolution_bitcast_fusion = f32[1,384,1536]{2,1,0:T(8,128)} fusion(bf16[1536,1024]{0,1:T(8,128)(2,1)S(1)} %fusion.6, f32[384,1024]{1,0:T(8,128)S(1)} %get-tuple-element.15, f32[384]{0:T(512)S(1)} %reduce.1, f32[1024]{0:T(1024)S(1)} %add_rsqrt_fusion, f32[1024]{0:T(1024)S(1)} %broadcast_multiply_fusion.2), kind=kOutput, calls=%fused_computation.12 | convolution fusion | flops 1209532416 | bytes 7087616 | tf_op jit(solution)/shard_map/cp,hp->ch/dot_general | solution.py:126
  64.8 4.5 %fusion.14 = (f32[384]{0:T(512)S(1)}, f32[1024]{0:T(1024)S(1)}, f32[1024]{0:T(1024)S(1)}, f32[1024,384]{0,1:T(8,128)S(1)}) fusion(f32[384,1024]{1,0:T(8,128)} %copy-done.1, f32[1024]{0:T(1024)S(1)} %add_rsqrt_fusion, f32[1024]{0:T(1024)S(1)} %broadcast_multiply_fusion.2, f32[384]{0:T(512)S(1)} %reduce.1, bf16[1536,1024]{0,1:T(8,128)(2,1)} %copy-done.16, ...), kind=kOutput, calls=%fused_computation.22 | convolution fusion | flops 1211102848 | bytes 7490560 | tf_op jit(solution)/shard_map/dot_general | solution.py:127
  69.4 0.6 convert_add_fusion
  69.9 0.9 fusion.27
  70.9 0.3 convolution_convert_fusion
  71.1 0.2 copy.40
  71.3 21.0 %all_to_all.19 = bf16[128,8,128]{2,1,0:T(8,128)(2,1)S(1)} all-to-all(bf16[128,8,128]{2,1,0:T(8,128)(2,1)S(1)} %copy.40), channel_id=1, replica_groups=mesh['groups'=2,'tiles'=8,'comp'=2] {'tiles'}, dimensions={0} | all-to-all | bytes 524288 | tf_op jit(solution)/shard_map/all_to_all | solution.py:38
  92.5 1.4 convolution_bitcast_fusion.2
  93.9 0.1 collective-permute-done.2
  94.0 0.2 convolution_convert_fusion.1
  94.2 0.7 fusion.24
  94.9 0.2 fusion.29
  95.1 0.3 convolution_bitcast_fusion.3
  95.4 36.0 %all-reduce = (f32[1,384]{1,0:T(1,128)}, f32[1,8,384]{2,1,0:T(8,128)}, f32[1,384,8]{1,2,0:T(8,128)}) all-reduce(f32[1,384]{1,0:T(1,128)S(1)} %broadcast_in_dim.57, f32[1,8,384]{2,1,0:T(8,128)S(1)} %convolution_bitcast_fusion.3, f32[1,384,8]{1,2,0:T(8,128)S(1)} %convolution_bitcast_fusion.2), channel_id=1, replica_groups=mesh['groups'=2,'tiles'=8,'comp'=2] {'tiles'}, use_global_device_ids=true, to_apply=%region_10.11 | all-reduce | flops 6528 | bytes 52224 | tf_op jit(solution)/shard_map/psum | solution.py:164
  131.4 3.0 %fusion.13 = f32[1,384,1024]{2,1,0:T(8,128)} fusion(f32[384,1024]{1,0:T(8,128)} %copy-done.3, bf16[1,8,8,128]{3,2,1,0:T(8,128)(2,1)S(1)} %fusion.29, bf16[1,8,384]{2,1,0:T(8,128)(2,1)S(1)} %copy-done.10), kind=kOutput, calls=%fused_computation.19 | convolution fusion | flops 6684672 | bytes 3168256 | tf_op jit(solution)/shard_map/kc,kp->cp/dot_general | solution.py:161
  134.4 105.6 %all-reduce.4.cloned.1.call-done = (f32[1,384,1536]{2,1,0:T(8,128)}, f32[1,1536,384]{2,1,0:T(8,128)}) async-done(((f32[1,384,1536]{2,1,0:T(8,128)}, f32[1,1536,384]{2,1,0:T(8,128)}), (f32[1,384,1536]{2,1,0:T(8,128)}, f32[1,1536,384]{2,1,0:T(8,128)})) %all-reduce.4.cloned.1.call-update) | async-done | bytes 4718608 | tf_op jit(solution)/shard_map/psum | solution.py:164
  239.9 3.4 %copy.82 = f32[1,384,1536]{2,1,0:T(8,128)} copy(f32[1,384,1536]{2,1,0:T(8,128)} %get-tuple-element.20) | data formatting | bytes 4718592
  243.3 1.4 copy.83
  (43 shorter events, 0.3 us)
Async XLA Ops:
  7.2 5.4 %copy-start = (bf16[1,64,128,128]{3,2,1,0:T(8,128)(2,1)S(1)}, bf16[1,64,128,128]{3,2,1,0:T(8,128)(2,1)}, u32[]{:S(2)}) copy-start(bf16[1,64,128,128]{3,2,1,0:T(8,128)(2,1)} %param.25) | copy-start | bytes 6291460
  12.6 2.2 copy-start.15
  13.8 20.5 %copy-start.13 = (f32[1,384]{1,0:T(1,128)S(1)}, f32[1,384]{1,0:T(1,128)}, u32[]{:S(2)}) copy-start(f32[1,384]{1,0:T(1,128)} %param.17) | copy-start | bytes 4612
  13.8 20.5 %copy-start.11 = (s32[1024]{0:T(1024)S(1)}, s32[1024]{0:T(1024)}, u32[]{:S(2)}) copy-start(s32[1024]{0:T(1024)} %param.20) | copy-start | bytes 12292
  13.8 34.2 %copy-start.4 = (bf16[1,384,1024]{2,1,0:T(8,128)(2,1)S(1)}, bf16[1,384,1024]{2,1,0:T(8,128)(2,1)}, u32[]{:S(2)}) copy-start(bf16[1,384,1024]{2,1,0:T(8,128)(2,1)} %param.13) | copy-start | bytes 2359300
  13.8 34.2 %copy-start.9 = (f32[1,384,8]{1,2,0:T(8,128)S(1)}, f32[1,384,8]{1,2,0:T(8,128)}, u32[]{:S(2)}) copy-start(f32[1,384,8]{1,2,0:T(8,128)} %param.19) | copy-start | bytes 36868
  14.3 9.9 %collective-permute-start = (f32[128,8,128]{2,0,1:T(8,128)S(1)}, f32[128,8,128]{2,0,1:T(8,128)}, u32[]{:S(2)}, u32[]{:S(2)}) collective-permute-start(f32[128,8,128]{2,0,1:T(8,128)S(1)} %fusion.39), channel_id=1, source_target_pairs={{0,1},{1,0},{2,3},{3,2},{4,5},{5,4},{6,7},{7,6},{8,9},{9,8},{10,11... | collective-permute-start | bytes 1572872 | tf_op jit(solution)/shard_map/ppermute | solution.py:13
  14.9 1.4 collective-permute-start.1
  17.0 13.5 %all-to-all-start.1 = ((s32[8,16,1]{1,2,0:T(1,128)}), s32[8,16,1]{1,2,0:T(1,128)S(1)}, u32[]{:S(2)}, u32[]{:S(2)}) async-start(s32[8,16,1]{1,2,0:T(1,128)} %bitcast.10), calls=%async_computation.1 | async-start | bytes 8192 | tf_op jit(solution)/shard_map/all_to_all | solution.py:29
  30.6 17.1 %all-to-all-start = ((f32[128,8,128]{2,1,0:T(8,128)}), f32[128,8,128]{2,1,0:T(8,128)S(1)}, u32[]{:S(2)}, u32[]{:S(2)}) async-start(f32[128,8,128]{2,1,0:T(8,128)} %copy.36), calls=%async_computation | async-start | bytes 1048576 | tf_op jit(solution)/shard_map/all_to_all | solution.py:28
  34.1 205.9 %all-reduce.4.cloned.1.call-start = ((), (), s32[]{:S(2)}) async-start(), calls=%async_computation.3 | async-start | bytes 9437184 | tf_op jit(solution)/shard_map/psum | solution.py:164
  48.0 1.8 copy-start.6
  49.6 10.7 %copy-start.1 = (f32[384,1024]{1,0:T(8,128)}, f32[384,1024]{1,0:T(8,128)S(1)}, u32[]{:S(2)}) copy-start(f32[384,1024]{1,0:T(8,128)S(1)} %get-tuple-element.15) | copy-start | bytes 4718596
  49.8 1.9 copy-start.7
  51.8 3.5 %copy-start.14 = (bf16[1,1536,384]{2,1,0:T(8,128)(2,1)S(1)}, bf16[1,1536,384]{2,1,0:T(8,128)(2,1)}, u32[]{:S(2)}) copy-start(bf16[1,1536,384]{2,1,0:T(8,128)(2,1)} %param.16) | copy-start | bytes 3538948
  60.3 1.7 copy-start.16
  64.8 4.5 %copy-start.2 = (f32[384,1024]{1,0:T(8,128)S(1)}, f32[384,1024]{1,0:T(8,128)}, u32[]{:S(2)}) copy-start(f32[384,1024]{1,0:T(8,128)} %copy-done.1) | copy-start | bytes 4718596
  64.8 4.5 %copy-start.8 = (bf16[1,384,1024]{2,1,0:T(8,128)(2,1)S(1)}, bf16[1,384,1024]{2,1,0:T(8,128)(2,1)}, u32[]{:S(2)}) copy-start(bf16[1,384,1024]{2,1,0:T(8,128)(2,1)} %param.14) | copy-start | bytes 2359300
  69.9 22.5 %copy-start.3 = (f32[384,1024]{1,0:T(8,128)}, f32[384,1024]{1,0:T(8,128)S(1)}, u32[]{:S(2)}) copy-start(f32[384,1024]{1,0:T(8,128)S(1)} %convert_add_fusion) | copy-start | bytes 4718596
  92.4 1.6 collective-permute-start.2
  93.9 1.0 copy-start.12
  94.2 37.2 %copy-start.10 = (bf16[1,8,384]{2,1,0:T(8,128)(2,1)S(1)}, bf16[1,8,384]{2,1,0:T(8,128)(2,1)}, u32[]{:S(2)}) copy-start(bf16[1,8,384]{2,1,0:T(8,128)(2,1)} %param.18) | copy-start | bytes 18436
  239.9 3.4 %copy-start.5 = (f32[1,1536,384]{2,1,0:T(8,128)S(1)}, f32[1,1536,384]{2,1,0:T(8,128)}, u32[]{:S(2)}) copy-start(f32[1,1536,384]{2,1,0:T(8,128)} %get-tuple-element.21) | copy-start | bytes 7077892
Sparse Core Ops, SparseCore 0:
  64.9 174.9 all-reduce.3
where the time goes:
time: 252 us
  waiting for transfers between devices  123 us (49%)
  blocking collectives  57 us (23%)
  matrix products  30.5 us (12%)
  between operations  14.3 us (6%)
  starting transfers between devices  11.6 us (5%)
  local copies, waits for them, and re-layouts  10.2 us (4%)
  other arithmetic  4.7 us (2%)
    psum x1, waiting for transfers between devices, body(): lax.psum((g_in, g_out, g_gain, g_export, g_lift), 'tiles')  106 us
    psum x1, blocking collectives, body(): lax.psum((g_in, g_out, g_gain, g_export, g_lift), 'tiles')  36 us
    all_to_all x1, blocking collectives, adjoint_across_tiles(): lax.all_to_all(values, 'tiles', split_axis=0, concat_axis=0, tiled=True)  21 us
    all_to_all x1, waiting for transfers between devices, slots_across_tiles(): lax.all_to_all(values, 'tiles', split_axis=0, concat_axis=0, tiled=True)  12.1 us
    all_to_all x1, starting transfers between devices, slots_across_tiles(): lax.all_to_all(block_ids, 'tiles', split_axis=0, concat_axis=0, tiled=True)  7.14 us
    unnamed x36, local copies, waits for them, and re-layouts  6.54 us
  transfers between devices with their start and end apart: 6, of which 5 were waited for; matrix products, arithmetic and copies ran while one was open for 6% of the time, Pallas kernels for 0%

commit v1 on v0

--- a/solution.py
+++ b/solution.py
@@ -1,6 +1,10 @@
+import functools
+
 import jax
 import jax.numpy as jnp
 from jax import lax
+from jax.experimental import pallas as pl
+from jax.experimental.pallas import tpu as pltpu
 from jax.sharding import PartitionSpec as P
 
 norm_eps = 1e-05
@@ -42,7 +46,7 @@
     return swapped(values, "comp", 0)
 
 
-def body(
+def general_body(
     state_field,
     cotangent,
     w_in,
@@ -167,6 +171,488 @@
     return (grad_local[None], g_in[None], g_out[None], g_gain[None], g_export[None], g_lift[None])
 
 
+MESH = pl.DeviceIdType.MESH
+SUB = 2
+NT = (((1,), (1,)), ((), ()))
+
+
+def ring_place(tile, count):
+    row, column = lax.div(tile, 2), lax.rem(tile, 2)
+    return jnp.where(column == 0, row, count - 1 - row)
+
+
+def ring_tile(place, count):
+    return jnp.where(place < count // 2, 2 * place, 2 * (count - 1 - place) + 1)
+
+
+def fused_kernel(
+    count,
+    spots_ref,
+    coef_ref,
+    partial_ref,
+    state_ref,
+    cot_ref,
+    keep_ref,
+    w_in_ref,
+    w_out_ref,
+    gain_ref,
+    lift_ref,
+    lift_t_ref,
+    export_t_ref,
+    weights_ref,
+    grads_ref,
+    small_ref,
+    gs_ref,
+    force_recv,
+    w_in_t,
+    masked,
+    d_active,
+    scaled,
+    normed,
+    inv_std,
+    forcing,
+    act,
+    d_hidden,
+    d_scaled,
+    own,
+    first,
+    ring,
+    df_send,
+    df_recv,
+    lower,
+    blocks,
+    small_send,
+    small_recv,
+    f_send,
+    f_recv,
+    a_send,
+    a_recv,
+    s_send,
+    s_recv,
+    rs_send,
+    rs_recv,
+    ag_send,
+    ag_recv,
+):
+    me = lax.axis_index("tiles")
+    comp = lax.axis_index("comp")
+    place = ring_place(me, count)
+    right = ring_tile(lax.rem(place + 1, count), count)
+    left = ring_tile(lax.rem(place + count - 1, count), count)
+    toward = (right, left)
+    channels, cells = state_ref.shape
+    rows = w_out_ref.shape[1]
+    piece = rows // SUB
+    half = cells // 2
+    fields = lift_ref.shape[1]
+    width = weights_ref.shape[-1]
+    per_tile = cells // width
+    block_cells = 256
+
+    def chunk(offset):
+        return lax.rem(place + offset + 2 * count, count)
+
+    def peer(step):
+        return lax.rem(me + step, count)
+
+    def source(step):
+        return lax.rem(me + count - step, count)
+
+    barrier = pltpu.get_barrier_semaphore()
+    for step in range(count):
+        pl.semaphore_signal(
+            barrier, inc=1, device_id={"tiles": peer(step), "comp": 1 - comp}, device_id_type=MESH
+        )
+        if step:
+            pl.semaphore_signal(
+                barrier, inc=1, device_id={"tiles": peer(step)}, device_id_type=MESH
+            )
+    pl.semaphore_wait(barrier, 2 * count - 1)
+
+    pending = []
+
+    def send(src, dst, send_sem, recv_sem, device):
+        copy = pltpu.make_async_remote_copy(
+            src_ref=src,
+            dst_ref=dst,
+            send_sem=send_sem,
+            recv_sem=recv_sem,
+            device_id=device,
+            device_id_type=MESH,
+        )
+        copy.start()
+        pending.append(copy)
+
+    def arrived(dst, send_sem, recv_sem):
+        pltpu.make_async_remote_copy(
+            src_ref=dst,
+            dst_ref=dst,
+            send_sem=send_sem,
+            recv_sem=recv_sem,
+            device_id={"tiles": right},
+            device_id_type=MESH,
+        ).wait_recv()
+
+    for step in range(count):
+        send(
+            partial_ref.at[peer(step)],
+            force_recv.at[me],
+            f_send.at[step],
+            f_recv.at[step],
+            {"tiles": peer(step), "comp": 1 - comp},
+        )
+
+    masked[...] = (cot_ref[...].astype(jnp.float32) * keep_ref[...]).astype(jnp.bfloat16)
+
+    @pl.loop(0, count)
+    def _(index):
+        d_active[index] = jnp.dot(
+            w_out_ref[index], masked[...], preferred_element_type=jnp.float32
+        )
+
+    for index in range(channels // 128):
+        span = slice(index * 128, (index + 1) * 128)
+        w_in_t[:, span] = w_in_ref[span, :].T
+
+    for step in range(count):
+        arrived(force_recv.at[source(step)], f_send.at[step], f_recv.at[step])
+    total = force_recv[0].astype(jnp.float32)
+    for index in range(1, count):
+        total = total + force_recv[index].astype(jnp.float32)
+    forcing[:, :half] = total[:fields]
+    forcing[:, half:] = total[fields:]
+
+    for start in range(0, cells, block_cells):
+        span = slice(start, start + block_cells)
+        summed_in = state_ref[:, span].astype(jnp.float32) + jnp.dot(
+            lift_ref[...], forcing[:, span], precision=highest, preferred_element_type=jnp.float32
+        )
+        centre = summed_in - jnp.mean(summed_in, axis=0, keepdims=True)
+        variance = jnp.mean(centre * centre, axis=0, keepdims=True)
+        inverse = 1.0 / jnp.sqrt(variance + norm_eps)
+        unit = centre * inverse
+        inv_std[:, span] = inverse
+        normed[:, span] = unit
+        scaled[:, span] = (gain_ref[...] * unit).astype(jnp.bfloat16)
+
+    def mlp(index):
+        at = pl.multiple_of(index * rows, 16)
+        w_rows = w_in_t[pl.ds(at, rows), :]
+        for start in range(0, cells, block_cells):
+            span = slice(start, start + block_cells)
+            hidden = jnp.dot(w_rows, scaled[:, span], preferred_element_type=jnp.float32)
+            gelu_value, gelu_slope = gelu_parts(hidden)
+            act[:, span] = gelu_value.astype(jnp.bfloat16)
+            d_hidden[index, :, span] = (d_active[index, :, span] * gelu_slope).astype(jnp.bfloat16)
+        own[0, index] = lax.dot_general(
+            act[...], masked[...], NT, preferred_element_type=jnp.float32
+        )
+        own[1, index] = lax.dot_general(
+            d_hidden[index], scaled[...], NT, preferred_element_type=jnp.float32
+        )
+
+    signs = (-1, 1)
+
+    def reduce_step(step):
+        for sub in range(SUB):
+            span = pl.ds(sub * piece, piece)
+            for way in range(2):
+                at = ring.at[way, step, span]
+                arrived(at, rs_send.at[way, step, sub], rs_recv.at[way, step, sub])
+                index = chunk(signs[way] * (step + 1))
+                value = ring[way, step, span].astype(jnp.float32) + own[way, index, span]
+                if step < count - 2:
+                    ring[way, step, span] = value.astype(jnp.bfloat16)
+                    send(
+                        at,
+                        ring.at[way, step + 1, span],
+                        rs_send.at[way, step + 1, sub],
+                        rs_recv.at[way, step + 1, sub],
+                        {"tiles": toward[way]},
+                    )
+                else:
+                    grads_ref[way, index, span] = value.astype(jnp.bfloat16)
+                    gather_send(0, sub, way)
+
+    def gather_send(step, sub, way):
+        at = grads_ref.at[way, chunk(signs[way] * (step - 1)), pl.ds(sub * piece, piece)]
+        send(
+            at,
+            at,
+            ag_send.at[way, step, sub],
+            ag_recv.at[way, step, sub],
+            {"tiles": toward[way]},
+        )
+
+    def gather_step(step):
+        for sub in range(SUB):
+            for way in range(2):
+                at = grads_ref.at[way, chunk(signs[way] * step), pl.ds(sub * piece, piece)]
+                arrived(at, ag_send.at[way, step, sub], ag_recv.at[way, step, sub])
+                if step < count - 2:
+                    gather_send(step + 1, sub, way)
+
+    mlp(place)
+    for sub in range(SUB):
+        span = pl.ds(sub * piece, piece)
+        for way in range(2):
+            first[way, span] = own[way, place, span].astype(jnp.bfloat16)
+            send(
+                first.at[way, span],
+                ring.at[way, 0, span],
+                rs_send.at[way, 0, sub],
+                rs_recv.at[way, 0, sub],
+                {"tiles": toward[way]},
+            )
+    for step in range(1, count // 2):
+
+        @pl.loop(0, 2)
+        def _(side):
+            mlp(chunk(jnp.where(side == 0, -step, step)))
+
+        reduce_step(step - 1)
+    mlp(chunk(count // 2))
+    reduce_step(count // 2 - 1)
+
+    gain = gain_ref[...]
+    for start in range(0, cells, block_cells):
+        span = slice(start, start + block_cells)
+        grad = jnp.dot(
+            w_in_ref[...],
+            d_hidden[:, :, span].reshape(count * rows, block_cells),
+            preferred_element_type=jnp.float32,
+        )
+        unit = normed[:, span]
+        weighted = grad * gain
+        product = weighted * unit
+        d_summed = inv_std[:, span] * (
+            weighted
+            - jnp.mean(weighted, axis=0, keepdims=True)
+            - unit * jnp.mean(product, axis=0, keepdims=True)
+        ) + masked[:, span].astype(jnp.float32)
+        d_scaled[:, span] = grad * unit
+        gs_ref[:, span] = d_summed
+        lowered = jnp.dot(
+            lift_t_ref[...], d_summed, precision=highest, preferred_element_type=jnp.float32
+        )
+        row = 0 if start < half else fields
+        place_at = start % half
+        lower[row : row + fields, place_at : place_at + block_cells] = lowered
+        if start == block_cells:
+            reduce_step(count // 2)
+    df_send[...] = lower[...].astype(jnp.bfloat16)
+    for step in range(count):
+        send(
+            df_send,
+            df_recv.at[me],
+            a_send.at[step],
+            a_recv.at[step],
+            {"tiles": peer(step), "comp": 1 - comp},
+        )
+    reduce_step(count // 2 + 1)
+    small_send[0:8, :] = lax.dot_general(
+        jnp.ones((8, cells), jnp.float32),
+        d_scaled[...],
+        NT,
+        precision=highest,
+        preferred_element_type=jnp.float32,
+    )
+    small_send[16:24, :] = lax.dot_general(
+        forcing[...], gs_ref[...], NT, precision=highest, preferred_element_type=jnp.float32
+    )
+    reduce_step(count // 2 + 2)
+
+    for step in range(count):
+        arrived(df_recv.at[source(step)], a_send.at[step], a_recv.at[step])
+    gather_step(0)
+    half_blocks = per_tile // 2
+    for index in range(count):
+        landed = df_recv[index].astype(jnp.float32)
+        for block in range(per_tile):
+            row = block // half_blocks * fields
+            column = block % half_blocks * width
+            blocks[index * per_tile + block] = landed[row : row + fields, column : column + width]
+
+    slots = weights_ref.shape[0]
+    parts = 4
+    sums = tuple(jnp.zeros((fields, width), jnp.float32) for _ in range(per_tile))
+    for part in range(parts):
+
+        def slot_body(slot, carry):
+            force = blocks[spots_ref[slot]].astype(jnp.bfloat16)
+            pulled = jnp.dot(force, weights_ref[slot], preferred_element_type=jnp.float32)
+            return tuple(
+                carry[block] + pulled * coef_ref[slot * per_tile + block]
+                for block in range(per_tile)
+            )
+
+        span = slots // parts
+        sums = lax.fori_loop(part * span, (part + 1) * span, slot_body, sums, unroll=4)
+        if part < 2:
+            gather_step(part + 1)
+    d_exported = jnp.concatenate(sums, axis=1).astype(jnp.bfloat16)
+    small_send[8:16, :] = lax.dot_general(
+        d_exported, state_ref[...], NT, preferred_element_type=jnp.float32
+    )
+    for step in range(1, count):
+        send(
+            small_send,
+            small_recv.at[me],
+            s_send.at[step],
+            s_recv.at[step],
+            {"tiles": peer(step)},
+        )
+    gather_step(3)
+    for start in range(0, cells, block_cells):
+        span = slice(start, start + block_cells)
+        gs_ref[:, span] += jnp.dot(
+            export_t_ref[...], d_exported[:, span], preferred_element_type=jnp.float32
+        )
+    for step in range(4, count - 1):
+        gather_step(step)
+    small_recv[me] = small_send[...]
+    for step in range(1, count):
+        arrived(small_recv.at[source(step)], s_send.at[step], s_recv.at[step])
+    total_small = small_recv[0]
+    for index in range(1, count):
+        total_small = total_small + small_recv[index]
+    small_ref[...] = total_small
+    for copy in pending:
+        copy.wait_send()
+
+
+def fused_body(
+    state_field,
+    cotangent,
+    w_in,
+    w_out,
+    norm_gain,
+    export_weight,
+    lift_weight,
+    wet_mask,
+    remap_tile,
+    source_block,
+    target_block,
+    slot_alive,
+    remap_weights,
+):
+    count = lax.axis_size("tiles")
+    state_local = state_field[0]
+    weights_local = remap_weights[0]
+    targets = remap_tile[0, :, 0]
+    alive_local = slot_alive[0].astype(jnp.float32)
+    channels, cells = state_local.shape
+    hidden_size = w_in.shape[2]
+    fields = export_weight.shape[1]
+    width = weights_local.shape[-1]
+    per_tile = cells // width
+    slots = weights_local.shape[0]
+    half = cells // 2
+    rows = hidden_size // count
+    exported = jnp.dot(
+        export_weight[0], state_local, preferred_element_type=jnp.float32
+    ).astype(jnp.bfloat16)
+    pick_source = source_block[0][:, None] == jnp.arange(per_tile, dtype=jnp.int32)[None, :]
+    source_rows = jnp.einsum(
+        "lb,kbp->lkp",
+        pick_source.astype(jnp.bfloat16),
+        exported.reshape(fields, per_tile, width),
+        preferred_element_type=jnp.float32,
+    ).astype(jnp.bfloat16)
+    products = jnp.einsum(
+        "lkp,lqp->lkq", source_rows, weights_local, preferred_element_type=jnp.float32
+    )
+    spots = targets * per_tile + target_block[0]
+    placing = jnp.where(
+        spots[None, :] == jnp.arange(count * per_tile, dtype=jnp.int32)[:, None],
+        alive_local[None, :],
+        0.0,
+    )
+    dense = jnp.einsum("sl,lkq->skq", placing, products, precision=highest).astype(jnp.bfloat16)
+    partial = (
+        dense.reshape(count, 2, per_tile // 2, fields, width)
+        .transpose(0, 1, 3, 2, 4)
+        .reshape(count, 2 * fields, half)
+    )
+    coef = (pick_source.astype(jnp.float32) * alive_local[:, None]).reshape(slots * per_tile)
+    is_ocean = lax.axis_index("comp") == 1
+    keep = jnp.where(is_ocean, (wet_mask > 0).astype(jnp.float32), 1.0)[None, :]
+    vmem = pl.BlockSpec(memory_space=pltpu.VMEM)
+    smem = pl.BlockSpec(memory_space=pltpu.SMEM)
+    steps = count - 1
+    f32, b16 = jnp.float32, jnp.bfloat16
+    dma = pltpu.SemaphoreType.DMA
+    grads, small, grad_state = pl.pallas_call(
+        functools.partial(fused_kernel, count),
+        out_shape=(
+            jax.ShapeDtypeStruct((2, count, rows, channels), b16),
+            jax.ShapeDtypeStruct((24, channels), f32),
+            jax.ShapeDtypeStruct((channels, cells), f32),
+        ),
+        in_specs=[smem] * 2 + [vmem] * 11,
+        out_specs=(vmem,) * 3,
+        scratch_shapes=[
+            pltpu.VMEM((count, 2 * fields, half), b16),
+            pltpu.VMEM((hidden_size, channels), b16),
+            pltpu.VMEM((channels, cells), b16),
+            pltpu.VMEM((count, rows, cells), f32),
+            pltpu.VMEM((channels, cells), b16),
+            pltpu.VMEM((channels, cells), f32),
+            pltpu.VMEM((1, cells), f32),
+            pltpu.VMEM((fields, cells), f32),
+            pltpu.VMEM((rows, cells), b16),
+            pltpu.VMEM((count, rows, cells), b16),
+            pltpu.VMEM((channels, cells), f32),
+            pltpu.VMEM((2, count, rows, channels), f32),
+            pltpu.VMEM((2, rows, channels), b16),
+            pltpu.VMEM((2, steps, rows, channels), b16),
+            pltpu.VMEM((2 * fields, half), b16),
+            pltpu.VMEM((count, 2 * fields, half), b16),
+            pltpu.VMEM((2 * fields, half), f32),
+            pltpu.VMEM((count * per_tile, fields, width), f32),
+            pltpu.VMEM((24, channels), f32),
+            pltpu.VMEM((count, 24, channels), f32),
+            dma((count,)),
+            dma((count,)),
+            dma((count,)),
+            dma((count,)),
+            dma((count,)),
+            dma((count,)),
+            dma((2, steps, SUB)),
+            dma((2, steps, SUB)),
+            dma((2, steps, SUB)),
+            dma((2, steps, SUB)),
+        ],
+        compiler_params=pltpu.CompilerParams(
+            collective_id=0, has_side_effects=True, vmem_limit_bytes=52 * 1024 * 1024
+        ),
+    )(
+        spots,
+        coef,
+        partial,
+        state_local,
+        cotangent[0],
+        keep,
+        w_in[0],
+        w_out[0].reshape(count, rows, channels),
+        norm_gain[0][:, None],
+        lift_weight[0],
+        lift_weight[0].T,
+        export_weight[0].T,
+        weights_local,
+    )
+    g_out = grads[0].reshape(hidden_size, channels).astype(f32)
+    g_in = grads[1].reshape(hidden_size, channels).T.astype(f32)
+    return (
+        grad_state[None],
+        g_in[None],
+        g_out[None],
+        small[0:1],
+        small[8:16][None],
+        small[16:24].T[None],
+    )
+
+
 def solution(mesh):
     placed = (
         P("comp", None, ("groups", "tiles")),
@@ -183,8 +669,9 @@
         P("comp", "tiles"),
         P("comp", "tiles", None, None),
     )
+    chosen = fused_body if mesh.shape["tiles"] == 8 else general_body
     return jax.shard_map(
-        body,
+        chosen,
         mesh=mesh,
         in_specs=placed,
         out_specs=(

time: 252 us -> 103 us (0.41)
  waiting for transfers between devices: 123 us -> 0 us
  Pallas kernels: 0 us -> 83 us
  blocking collectives: 57 us -> 0 us
  matrix products: 30.5 us -> 5.5 us
  between operations: 14.3 us -> 0.77 us
  starting transfers between devices: 11.6 us -> 0 us
    psum x1 -> x0, waiting for transfers between devices: 106 us -> none  [body(): lax.psum((g_in, g_out, g_gain, g_export, g_lift), 'tiles')]
    pallas_call x0 -> x1, Pallas kernels: none -> 83 us  [fused_body(): pl.pallas_call(functools.partial(fused_kernel, count), out_shape=(jax.Sha...]
    psum x1 -> x0, blocking collectives: 36 us -> none  [body(): lax.psum((g_in, g_out, g_gain, g_export, g_lift), 'tiles')]
    dot_general x19 -> x4, matrix products: 30.5 us -> 5.5 us  [the longest x1 2.76 us: fused_body(): jnp.einsum('lkp,lqp->lkq', source_rows, weights_local, preferred_element_...]
    all_to_all x1 -> x0, blocking collectives: 21 us -> none  [adjoint_across_tiles(): lax.all_to_all(values, 'tiles', split_axis=0, concat_axis=0, tiled=True)]
    all_to_all x2 -> x0, waiting for transfers between devices: 16.3 us -> none  [the longest x1 12.1 us: slots_across_tiles(): lax.all_to_all(values, 'tiles', split_axis=0, concat_axis=0, tiled=True)]
    all_to_all x2 -> x0, starting transfers between devices: 10.6 us -> none  [the longest x1 7.14 us: slots_across_tiles(): lax.all_to_all(block_ids, 'tiles', split_axis=0, concat_axis=0, tiled=True)]
    unnamed x36 -> x14, local copies, waits for them, and re-layouts: 6.54 us -> 1.33 us
  transfers between devices with their start and end apart: 6 -> 0, of which waited for: 5 -> 0; matrix products, arithmetic and copies ran while one was open for 6% -> 0% of each run, Pallas kernels for 0% -> 0%
where the time goes in v1:
time: 103 us; the launch traced here: 102 us
  Pallas kernels  83 us (81%)
  local copies, waits for them, and re-layouts  7.76 us (8%)
  matrix products  5.5 us (5%)
  other arithmetic  5.35 us (5%)
    pallas_call x1, Pallas kernels, fused_body(): pl.pallas_call(functools.partial(fused_kernel, count), out_shape=(jax.Sha...  83 us
    convert_element_type x1, other arithmetic, fused_body(): g_out = grads[0].reshape(hidden_size, channels).astype(f32)  2.95 us
    slice x1, local copies, waits for them, and re-layouts, fused_body(): g_out = grads[0].reshape(hidden_size, channels).astype(f32)  2.88 us
    dot_general x1, matrix products, fused_body(): jnp.einsum('lkp,lqp->lkq', source_rows, weights_local, preferred_element_...  2.76 us

profile of v1, /device:TPU:0, one launch (start us, length us, event | category | flops | bytes accessed | tf_op | source)
XLA Modules:
  0.0 102.4 jit_solution(4331001081865977711)
XLA Ops:
  0.6 0.7 bitcast_add_fusion.1.spots_ref
  1.3 0.7 fusion.15
  2.0 0.0 copy-start.4
  2.0 0.0 copy-start.5
  2.0 0.8 fusion.6
  2.8 0.1 mul.34.coef_ref
  2.9 0.0 copy-start.1
  2.9 0.0 copy-start.3
  2.9 1.4 %fusion = bf16[8,8,128]{2,0,1:T(8,128)(2,1)S(1)} fusion(bf16[1,8,384]{2,1,0:T(8,128)(2,1)} %param.18, bf16[1,384,1024]{2,1,0:T(8,128)(2,1)} %param.13), kind=kOutput, calls=%fused_computation.4 | convolution fusion | flops 6299648 | bytes 808960 | tf_op jit(solution)/shard_map/dot_general | solution.py:552
  4.3 0.0 copy-start
  4.3 1.0 fusion.7
  5.2 2.8 %fusion.2 = f32[64,8,128]{2,1,0:T(8,128)S(1)} fusion(bf16[64,8,128]{2,0,1:T(8,128)(2,1)S(1)} %fusion.7, bf16[1,64,128,128]{3,2,1,0:T(8,128)(2,1)} %param.25), kind=kOutput, calls=%fused_computation.7 | convolution fusion | flops 16777216 | bytes 2490368 | tf_op jit(solution)/shard_map/lkp,lqp->lkq/dot_general | solution.py:562
  8.0 0.4 convolution_convert_fusion
  8.4 0.1 copy.38
  8.5 0.0 copy-done.4
  8.5 0.0 copy-done.5
  8.5 0.1 copy.25.gain_ref
  8.7 0.0 copy-done.1
  8.7 0.1 copy.26.lift_ref
  8.8 0.0 copy-done.3
  8.8 0.2 copy.23
  9.0 0.0 copy-done
  9.0 83.0 %shard_map.172 = (bf16[2,8,192,384]{3,2,1,0:T(8,128)(2,1)}, f32[24,384]{1,0:T(8,128)S(1)}, f32[384,1024]{1,0:T(8,128)}) custom-call(s32[64]{0:T(128)S(1)} %bitcast_add_fusion.1.spots_ref, f32[512]{0:T(512)S(1)} %mul.34.coef_ref, bf16[8,16,512]{2,1,0:T(8,128)(2,1)S(1)} %bitcast.64, bf16[384,1024]{1,0:T(8,128)(2,1)S(1)} %bitcast.63, ...), custom_call_target="tpu_custom_call" | custom-call | tf_op jit(solution)/shard_map/pallas_call | solution.py:585
  92.0 2.9 %fusion.19 = (bf16[1,8,192,384]{3,2,1,0:T(8,128)(2,1)}, bf16[1,8,192,384]{3,2,1,0:T(8,128)(2,1)S(1)}) fusion(bf16[2,8,192,384]{3,2,1,0:T(8,128)(2,1)} %get-tuple-element.10), kind=kLoop, calls=%fused_computation.32 | loop fusion | bytes 4718592 | tf_op jit(solution)/shard_map/slice | solution.py:644
  94.9 0.3 bitcast_convert_fusion.1
  95.2 2.0 %copy.27 = f32[1536,384]{0,1:T(8,128)} copy(f32[1536,384]{1,0:T(8,128)S(1)} %bitcast_convert_fusion.1) | data formatting | bytes 4718592 | tf_op jit(solution)/shard_map/broadcast_in_dim | solution.py:648
  97.1 0.0 copy-start.2
  97.1 2.9 %bitcast_convert_fusion = f32[1,1536,384]{2,1,0:T(8,128)} fusion(bf16[1,8,192,384]{3,2,1,0:T(8,128)(2,1)} %get-tuple-element.12), kind=kLoop, calls=%fused_computation | loop fusion | flops 589824 | bytes 3538944 | tf_op jit(solution)/shard_map/convert_element_type | solution.py:644
  100.1 0.6 slice.17
  100.6 0.6 slice_bitcast_fusion
  101.2 0.0 copy-done.2
  101.2 1.1 %copy.40 = f32[1,384,1024]{2,1,0:T(8,128)} copy(f32[1,384,1024]{2,1,0:T(8,128)S(1)} %bitcast.71) | data formatting | bytes 3145728
  (1 shorter events, 0.0 us)
Async XLA Ops:
  2.0 6.5 %copy-start.4 = (s32[1024]{0:T(1024)S(1)}, s32[1024]{0:T(1024)}, u32[]{:S(2)}) copy-start(s32[1024]{0:T(1024)} %param.20) | copy-start | bytes 12292
  2.0 6.5 %copy-start.5 = (f32[1,384]{1,0:T(1,128)S(1)}, f32[1,384]{1,0:T(1,128)}, u32[]{:S(2)}) copy-start(f32[1,384]{1,0:T(1,128)} %param.17) | copy-start | bytes 4612
  2.9 5.8 %copy-start.1 = (f32[1,384,8]{1,2,0:T(8,128)S(1)}, f32[1,384,8]{1,2,0:T(8,128)}, u32[]{:S(2)}) copy-start(f32[1,384,8]{1,2,0:T(8,128)} %param.19) | copy-start | bytes 36868
  2.9 6.0 %copy-start.3 = (bf16[1,8,384]{2,1,0:T(8,128)(2,1)S(1)}, bf16[1,8,384]{2,1,0:T(8,128)(2,1)}, u32[]{:S(2)}) copy-start(bf16[1,8,384]{2,1,0:T(8,128)(2,1)} %param.18) | copy-start | bytes 18436
  4.3 4.7 %copy-start = (bf16[1,384,1024]{2,1,0:T(8,128)(2,1)S(1)}, bf16[1,384,1024]{2,1,0:T(8,128)(2,1)}, u32[]{:S(2)}) copy-start(bf16[1,384,1024]{2,1,0:T(8,128)(2,1)} %param.13) | copy-start | bytes 2359300
  97.1 4.1 %copy-start.2 = (f32[384,1024]{1,0:T(8,128)S(1)}, f32[384,1024]{1,0:T(8,128)}, u32[]{:S(2)}) copy-start(f32[384,1024]{1,0:T(8,128)} %get-tuple-element.9) | copy-start | bytes 4718596
